TPU v7x, 256 devices: a whole 4x4x8 slice. The times are simulated.
256 devices in a mesh: ed: 64 (over y, z, core), tp: 4 (over x).
Axes of the slice: x: 4, y: 4, z: 8, core: 2. Of those that a mesh axis runs over, the one named last changes fastest.
Arguments:
- layer_activations_input: bfloat16 [8192, 3072], P('ed', 'tp'), may hold values from -6 to 6
- output_gradient: bfloat16 [8192, 3072], P('ed', 'tp'), may hold values from -2 to 2
- specialist_choices_matrix: int32 [8192, 2], P('ed'), may hold values from 0 to 7, all different within a row
- mixing_coefficients: float32 [8192, 2], P('ed'), may hold values from 0.1 to 1
- quota_table: int32 [64, 8], P('ed'), may hold values from 4 to 12, as said below
- gating_matrix: bfloat16 [3072, 131072], P(None, ('ed', 'tp')), may hold values from -0.109375 to 0.109375
- widening_matrix: bfloat16 [3072, 131072], P(None, ('ed', 'tp')), may hold values from -0.109375 to 0.109375
- contracting_matrix: bfloat16 [131072, 3072], P(('ed', 'tp')), may hold values from -0.046875 to 0.046875
Outputs:
- token_grads: bfloat16 [8192, 3072], P('ed', 'tp')
- gate_grads: float32 [8192, 2], P('ed')
Inputs may be any that keep to these rules, and one draw needn't show every extreme that they name: quota_table[s, e] is a multiple of 4; in every source block one expert (a low capacity: most assignments are dropped, as if the layer saw many more tokens at capacity factor about 1) has capacity 12.
All inputs are finite; a program needn't handle non-finite values.
Results may differ from a plain program's by a relative error of at most 0.011.
Values may be sent and summed in bfloat16 or wider, within the bound.
No kernel may reach another device: no remote copies, remote signals or barrier semaphores. Data moves between devices by JAX's collectives and lax.ppermute only.
A program may use at most 128 MiB of HBM per device.

v0:
```python
import jax
import jax.numpy as jnp
from jax import lax
from jax.sharding import PartitionSpec as P

EXPERTS = 8
CAP = 12


def seat_positions(specialist_choices_matrix, capacity_row):
    flat_ids = specialist_choices_matrix.reshape(-1)
    onehot = (flat_ids[:, None] == jnp.arange(EXPERTS, dtype=jnp.int32)[None, :]).astype(jnp.int32)
    before = jnp.sum((jnp.cumsum(onehot, axis=0) - onehot) * onehot, axis=1)
    allowed = jnp.sum(onehot * capacity_row[None, :], axis=1)
    number = jnp.where(before < allowed, flat_ids * CAP + before, -1)
    return number.reshape(specialist_choices_matrix.shape)


def send_home(payload, replicas):
    returned = (
        lax.all_to_all(payload[0], "ed", split_axis=0, concat_axis=0, tiled=True),
        lax.all_to_all(payload[1], "ed", split_axis=0, concat_axis=0, tiled=True),
    )
    return tuple(
        (member.reshape((EXPERTS, replicas) + member.shape[1:]).sum(axis=1) for member in returned)
    )


def local(
    layer_activations_input,
    output_gradient,
    specialist_choices_matrix,
    mixing_coefficients,
    quota_table,
    gating_matrix,
    widening_matrix,
    contracting_matrix,
):
    replicas = lax.axis_size("ed") // EXPERTS
    tp_count = lax.axis_size("tp")
    slot_count = EXPERTS * CAP
    rank_numbers = seat_positions(specialist_choices_matrix, quota_table[0])
    matches = rank_numbers[None, :, :] == jnp.arange(slot_count, dtype=jnp.int32)[:, None, None]
    picker = jnp.any(matches, axis=2).astype(jnp.bfloat16)
    send_x = (
        jnp.dot(picker, layer_activations_input, preferred_element_type=jnp.float32)
        .astype(jnp.bfloat16)
        .reshape(EXPERTS, CAP, -1)
    )
    send_d = (
        jnp.dot(picker, output_gradient, preferred_element_type=jnp.float32)
        .astype(jnp.bfloat16)
        .reshape(EXPERTS, CAP, -1)
    )
    arrived = (
        lax.all_to_all(
            jnp.repeat(send_x, replicas, axis=0), "ed", split_axis=0, concat_axis=0, tiled=True
        ),
        lax.all_to_all(
            jnp.repeat(send_d, replicas, axis=0), "ed", split_axis=0, concat_axis=0, tiled=True
        ),
    )
    sources = arrived[0].shape[0]
    row_count = sources * CAP
    rows_x = arrived[0].reshape(row_count, -1)
    rows_d = arrived[1].reshape(row_count, -1)
    piece_x = lax.all_gather(rows_x, "tp", axis=1, tiled=True)
    piece_d = lax.all_gather(rows_d, "tp", axis=1, tiled=True)
    pre_gate = jnp.dot(piece_x, gating_matrix, preferred_element_type=jnp.float32)
    pre_up = jnp.dot(piece_x, widening_matrix, preferred_element_type=jnp.float32)
    back_act = lax.dot_general(
        piece_d, contracting_matrix, (((1,), (1,)), ((), ())), preferred_element_type=jnp.float32
    )
    sigmoid_gate = jax.nn.sigmoid(pre_gate)
    swish = pre_gate * sigmoid_gate
    activation = (swish * pre_up).astype(jnp.bfloat16)
    partial_dot = jnp.sum(activation.astype(jnp.float32) * back_act, axis=1)
    grad_gate = (back_act * pre_up * sigmoid_gate * (1.0 + pre_gate * (1.0 - sigmoid_gate))).astype(
        jnp.bfloat16
    )
    grad_up = (back_act * swish).astype(jnp.bfloat16)
    back_rows = jnp.dot(grad_gate, gating_matrix.T, preferred_element_type=jnp.float32) + jnp.dot(
        grad_up, widening_matrix.T, preferred_element_type=jnp.float32
    )
    spread_dot = jnp.broadcast_to(partial_dot[:, None], (row_count, tp_count))
    homed = send_home(
        (back_rows.reshape(sources, CAP, -1), spread_dot.reshape(sources, CAP, tp_count)), replicas
    )
    returned = (
        lax.psum_scatter(homed[0], "tp", scatter_dimension=2, tiled=True),
        lax.psum_scatter(homed[1], "tp", scatter_dimension=2, tiled=True),
    )
    slot_rows = returned[0].reshape(slot_count, -1)
    slot_dot = returned[1].reshape(slot_count)
    slot_weight = jnp.sum(jnp.where(matches, mixing_coefficients[None, :, :], 0.0), axis=2)
    token_sums = lax.dot_general(
        slot_weight,
        slot_rows,
        (((0,), (0,)), ((), ())),
        precision=lax.Precision.HIGHEST,
        preferred_element_type=jnp.float32,
    )
    gate_grads = jnp.sum(jnp.where(matches, slot_dot[:, None, None], 0.0), axis=0)
    return (token_sums.astype(jnp.bfloat16), gate_grads)


def solution(mesh):
    in_specs = (
        P("ed", "tp"),
        P("ed", "tp"),
        P("ed", None),
        P("ed", None),
        P("ed", None),
        P(None, ("ed", "tp")),
        P(None, ("ed", "tp")),
        P(("ed", "tp"), None),
    )
    out_specs = (P("ed", "tp"), P("ed", None))
    return jax.shard_map(local, mesh=mesh, in_specs=in_specs, out_specs=out_specs, check_vma=False)
```

profile of v0, /device:TPU:32, one launch (start us, length us, event | category | flops | bytes accessed | tf_op | source)
XLA Modules:
  0.0 533.9 jit_solution(16013121279712400671)
XLA Ops:
  7.2 0.9 copy.34
  9.3 0.8 select_reduce_fusion.2
  10.5 0.7 compare_select_fusion
  11.2 1.1 convolution_convert_fusion.1
  12.5 50.8 %all_to_all.20 = bf16[64,12,768]{2,1,0:T(8,128)(2,1)} all-to-all(bf16[64,12,768]{2,1,0:T(8,128)(2,1)S(1)} %bitcast.32), channel_id=1, replica_groups=mesh['ed'=64,'tp'=4] {'ed'}, dimensions={0} | all-to-all | bytes 2359296 | tf_op jit(solution)/shard_map/all_to_all | solution.py:56
  63.2 3.2 reshape.78
  66.9 45.8 %all_to_all.21 = bf16[64,12,768]{2,1,0:T(8,128)(2,1)} all-to-all(bf16[64,12,768]{2,1,0:T(8,128)(2,1)S(1)} %bitcast.33), channel_id=1, replica_groups=mesh['ed'=64,'tp'=4] {'ed'}, dimensions={0} | all-to-all | bytes 2359296 | tf_op jit(solution)/shard_map/all_to_all | solution.py:59
  112.7 3.1 reshape.75
  116.1 3.3 all-gather.5.cloned.1.call-done
  119.4 6.3 %fusion.11 = f32[768,512]{0,1:T(8,128)} fusion(bf16[768,3072]{1,0:T(8,128)(2,1)} %all-gather.5.cloned.1.call-done, bf16[3072,512]{1,0:T(8,128)(2,1)S(1)} %copy-done), kind=kOutput, calls=%fused_computation.31 | convolution fusion | flops 2415919104 | bytes 9437184 | tf_op jit(solution)/shard_map/dot_general | solution.py:69
  125.7 3.9 fusion.10
  129.7 47.2 %all-gather.3.cloned.1.call-done = bf16[768,3072]{1,0:T(8,128)(2,1)} async-done(((bf16[768,768]{1,0:T(8,128)(2,1)}), bf16[768,3072]{1,0:T(8,128)(2,1)}) %all-gather.3.cloned.1.call-update) | async-done | bytes 4718608 | tf_op jit(solution)/shard_map/all_gather | solution.py:68
  176.8 7.0 %multiply_reduce_fusion = (f32[768]{0:T(1024)S(1)}, f32[768,512]{0,1:T(8,128)S(1)}) fusion(f32[768,512]{0,1:T(8,128)} %fusion.10, f32[768,512]{0,1:T(8,128)} %fusion.11, bf16[768,3072]{1,0:T(8,128)(2,1)} %all-gather.3.cloned.1.call-done, bf16[512,3072]{1,0:T(8,128)(2,1)} %param.15), kind=kOutput, calls=%fused_computation.2 | convolution fusion | flops 2419457280 | bytes 12585984 | tf_op jit(solution)/shard_map/dot_general | solution.py:71
  183.9 3.1 fusion.1
  187.1 5.4 %convolution_add_fusion = f32[768,3072]{1,0:T(8,128)} fusion(f32[768,3072]{1,0:T(8,128)S(1)} %fusion.1, bf16[3072,512]{1,0:T(8,128)(2,1)S(1)} %copy-done.4, f32[768,512]{0,1:T(8,128)S(1)} %get-tuple-element.7, f32[768,512]{0,1:T(8,128)S(1)} %copy-done.2), kind=kOutput, calls=%fused_computation.1 | convolution fusion | flops 2420637696 | bytes 25165824 | tf_op jit(solution)/shard_map/dot_general | solution.py:82
  192.5 10.1 %reshape.79 = f32[64,12,3072]{2,1,0:T(8,128)} reshape(f32[768,3072]{1,0:T(8,128)} %convolution_add_fusion) | data formatting | bytes 18874368 | tf_op jit(solution)/shard_map/reshape | solution.py:87
  202.6 285.0 %all_to_all.22 = f32[64,12,3072]{2,1,0:T(8,128)S(1)} all-to-all(f32[64,12,3072]{2,1,0:T(8,128)} %reshape.79), channel_id=1, replica_groups=mesh['ed'=64,'tp'=4] {'ed'}, dimensions={0} | all-to-all | bytes 18874368 | tf_op jit(solution)/shard_map/all_to_all | solution.py:21
  487.6 2.3 bitcast_reduce_fusion
  490.0 0.7 broadcast_in_dim.51
  490.7 7.4 %all-to-all-start.3 = ((f32[64,12,4]{1,2,0:T(4,128)}), f32[64,12,4]{1,2,0:T(4,128)S(1)}, u32[]{:S(2)}, u32[]{:S(2)}) async-start(f32[64,12,4]{1,2,0:T(4,128)} %broadcast_in_dim.51), calls=%async_computation.4 | async-start | bytes 262144 | tf_op jit(solution)/shard_map/all_to_all | solution.py:22
  498.7 9.4 %all-to-all-done.3 = f32[64,12,4]{1,2,0:T(4,128)S(1)} async-done(((f32[64,12,4]{1,2,0:T(4,128)}), f32[64,12,4]{1,2,0:T(4,128)S(1)}, u32[]{:S(2)}, u32[]{:S(2)}) %all-to-all-start.3) | async-done | bytes 12320 | tf_op jit(solution)/shard_map/all_to_all | solution.py:22
  508.2 15.5 %all-reduce = f32[8,12,4]{1,0,2:T(8,128)S(1)} all-reduce(f32[8,12,4]{1,0,2:T(8,128)S(1)} %copy.39), channel_id=3, replica_groups=mesh['ed'=64,'tp'=4] {'tp'}, use_global_device_ids=true, to_apply=%region_10.11.clone | all-reduce | flops 384 | bytes 3072
  525.1 1.0 reshape.81
  526.2 1.2 convolution_convert_fusion
  (51 shorter events, 4.5 us)
Async XLA Ops:
  7.2 112.2 %copy-start = (bf16[3072,512]{1,0:T(8,128)(2,1)S(1)}, bf16[3072,512]{1,0:T(8,128)(2,1)}, u32[]{:S(2)}) copy-start(bf16[3072,512]{1,0:T(8,128)(2,1)} %param.13) | copy-start | bytes 9437188
  7.2 112.2 %all-gather.5.cloned.1.call-start = ((), (), s32[]{:S(2)}) async-start(), calls=%async_computation.6 | async-start | bytes 5898240 | tf_op jit(solution)/shard_map/all_gather | solution.py:67
  63.2 3.3 copy-start.6
  66.4 110.4 %all-gather.3.cloned.1.call-start = ((), (), s32[]{:S(2)}) async-start(), calls=%async_computation.5 | async-start | bytes 5898240 | tf_op jit(solution)/shard_map/all_gather | solution.py:68
  115.8 409.3 %reduce-scatter.2.cloned.1.call-start = ((), (), s32[]{:S(2)}) async-start(), calls=%async_computation.7 | async-start | bytes 1966080 | tf_op jit(solution)/shard_map/reduce_scatter | solution.py:90
  119.4 6.3 %copy-start.3 = (bf16[3072,512]{1,0:T(8,128)(2,1)S(1)}, bf16[3072,512]{1,0:T(8,128)(2,1)}, u32[]{:S(2)}) copy-start(bf16[3072,512]{1,0:T(8,128)(2,1)} %param.14) | copy-start | bytes 9437188
  119.4 6.3 %copy-start.8 = (bf16[768,3072]{1,0:T(8,128)(2,1)S(1)}, bf16[768,3072]{1,0:T(8,128)(2,1)}, u32[]{:S(2)}) copy-start(bf16[768,3072]{1,0:T(8,128)(2,1)} %all-gather.5.cloned.1.call-done) | copy-start | bytes 14155780
  176.8 7.1 %copy-start.2 = (f32[768,512]{0,1:T(8,128)S(1)}, f32[768,512]{0,1:T(8,128)}, u32[]{:S(2)}) copy-start(f32[768,512]{0,1:T(8,128)} %fusion.11) | copy-start | bytes 4718596
  176.8 7.1 %copy-start.5 = (f32[768,512]{0,1:T(8,128)S(1)}, f32[768,512]{0,1:T(8,128)}, u32[]{:S(2)}) copy-start(f32[768,512]{0,1:T(8,128)} %fusion.10) | copy-start | bytes 4718596
  183.9 3.1 copy-start.4
  489.9 8.2 %copy-start.9 = (u32[256]{0:T(256)S(1)}, u32[256]{0:T(256)}, u32[]{:S(2)}) copy-start(u32[256]{0:T(256)} %constant.20) | copy-start | bytes 3076
  489.9 34.6 %copy-start.7 = (f32[128,2]{0,1:T(2,128)S(1)}, f32[128,2]{0,1:T(2,128)}, u32[]{:S(2)}) copy-start(f32[128,2]{0,1:T(2,128)} %param.11) | copy-start | bytes 3076
  489.9 37.5 %copy-start.1 = (bf16[3072,512]{1,0:T(8,128)(2,1)S(1)}, bf16[3072,512]{1,0:T(8,128)(2,1)}, u32[]{:S(2)}) copy-start(bf16[3072,512]{1,0:T(8,128)(2,1)} %param.13) | copy-start | bytes 9437188
  490.7 17.4 %all-to-all-start.3 = ((f32[64,12,4]{1,2,0:T(4,128)}), f32[64,12,4]{1,2,0:T(4,128)S(1)}, u32[]{:S(2)}, u32[]{:S(2)}) async-start(f32[64,12,4]{1,2,0:T(4,128)} %broadcast_in_dim.51), calls=%async_computation.4 | async-start | bytes 262144 | tf_op jit(solution)/shard_map/all_to_all | solution.py:22
Sparse Core Ops, SparseCore 0:
  66.6 52.7 all-gather.4
  121.2 55.5 all-gather.2
  490.1 25.5 reduce-scatter.1
where the time goes:
time: 535 us; the launch traced here: 534 us
  blocking collectives  397 us (74%)
  waiting for transfers between devices  60 us (11%)
  matrix products  28.4 us (5%)
  local copies, waits for them, and re-layouts  21.7 us (4%)
  between operations  13.9 us (3%)
  starting transfers between devices  7.71 us (1%)
    all_to_all x1, blocking collectives, send_home(): lax.all_to_all(payload[0], 'ed', split_axis=0, concat_axis=0, tiled=True)  285 us
    all_to_all x1, blocking collectives, local(): lax.all_to_all(jnp.repeat(send_x, replicas, axis=0), 'ed', split_axis=0,...  50.8 us
    all_gather x1, waiting for transfers between devices, local(): piece_d = lax.all_gather(rows_d, 'tp', axis=1, tiled=True)  47.2 us
    all_to_all x1, blocking collectives, local(): lax.all_to_all(jnp.repeat(send_d, replicas, axis=0), 'ed', split_axis=0,...  45.8 us
    unnamed x1, blocking collectives  15.5 us
  transfers between devices with their start and end apart: 4, of which 3 were waited for; matrix products, arithmetic and copies ran while one was open for 3% of the time, Pallas kernels for 0%

commit v1 on v0

v1 whole, which is shorter than its diff:
```python
import functools

import jax
import jax.numpy as jnp
from jax import lax
from jax.experimental import pallas as pl
from jax.experimental.pallas import tpu as pltpu
from jax.sharding import PartitionSpec as P

EXPERTS = 8
CAP = 12
PAD = 16
SLOTS = EXPERTS * CAP
BLOCK = 768
GROUPS = ((0, 1, 2, 3),)
OFFSETS = (0, 3, 1, 2)
HIDDEN_STEP = 256


def seat_positions(specialist_choices_matrix, capacity_row):
    flat_ids = specialist_choices_matrix.reshape(-1)
    onehot = (flat_ids[:, None] == jnp.arange(EXPERTS, dtype=jnp.int32)[None, :]).astype(jnp.int32)
    before = jnp.sum((jnp.cumsum(onehot, axis=0) - onehot) * onehot, axis=1)
    allowed = jnp.sum(onehot * capacity_row[None, :], axis=1)
    number = jnp.where(before < allowed, flat_ids * PAD + before, -1)
    return number.reshape(specialist_choices_matrix.shape)


def along_x(value, step):
    return lax.ppermute(value, "tp", [(i, (i + step) % 4) for i in range(4)])


def along_z(value, flip):
    return lax.ppermute(value, "ed", [(i, i ^ (flip * 2)) for i in range(64)])


def across_cores(value):
    return lax.ppermute(value, "ed", [(i, i ^ 1) for i in range(64)])


def among_experts(value):
    groups = [[expert * 8 + place for expert in range(EXPERTS)] for place in range(8)]
    return lax.all_to_all(
        value, "ed", split_axis=0, concat_axis=0, tiled=True, axis_index_groups=groups
    )


def expert_body(pieces, place_ref, *refs):
    piece_refs = refs[: 5 * pieces]
    weights = (refs[5 * pieces : 5 * pieces + 3], refs[5 * pieces + 3 : 5 * pieces + 6])
    outs = refs[5 * pieces + 6 : 5 * pieces + 10]
    dot_ref = refs[5 * pieces + 10]
    xs, ys, acc = refs[5 * pieces + 11 :]
    step = pl.program_id(0)

    @pl.when(step == 0)
    def _():
        for piece in range(pieces):
            own, left, right, far_x, far_d = piece_refs[5 * piece : 5 * piece + 5]
            rows = pl.ds(piece * SLOTS, SLOTS)
            for k, block in enumerate((own, left, right)):
                xs[k, rows, :] = block[:SLOTS, :]
                ys[k, rows, :] = block[SLOTS:, :]
            xs[3, rows, :] = far_x[...]
            ys[3, rows, :] = far_d[...]
        dot_ref[...] = jnp.zeros_like(dot_ref)

    place = place_ref[0]
    starts = [pl.multiple_of(((place + off) % 4) * BLOCK, BLOCK) for off in OFFSETS]
    f32 = jnp.float32
    transposed = (((1,), (1,)), ((), ()))
    grads = []
    dots = dot_ref[...]
    for gate_ref, up_ref, down_ref in weights:
        pre_gate = sum(
            jnp.dot(xs[k], gate_ref[pl.ds(starts[k], BLOCK), :], preferred_element_type=f32)
            for k in range(4)
        )
        pre_up = sum(
            jnp.dot(xs[k], up_ref[pl.ds(starts[k], BLOCK), :], preferred_element_type=f32)
            for k in range(4)
        )
        back_act = sum(
            lax.dot_general(
                ys[k], down_ref[:, pl.ds(starts[k], BLOCK)], transposed, preferred_element_type=f32
            )
            for k in range(4)
        )
        sigmoid_gate = jax.nn.sigmoid(pre_gate)
        swish = pre_gate * sigmoid_gate
        activation = (swish * pre_up).astype(jnp.bfloat16)
        product = activation.astype(f32) * back_act
        for lane in range(HIDDEN_STEP // 128):
            dots = dots + product[:, lane * 128 : (lane + 1) * 128]
        grads.append(
            (
                (back_act * pre_up * sigmoid_gate * (1.0 + pre_gate * (1.0 - sigmoid_gate))).astype(
                    jnp.bfloat16
                ),
                (back_act * swish).astype(jnp.bfloat16),
            )
        )
    dot_ref[...] = dots
    last = pl.num_programs(0) - 1
    for k in (3, 1, 2, 0):
        total = None
        for (grad_gate, grad_up), (gate_ref, up_ref, _) in zip(grads, weights):
            term = lax.dot_general(
                grad_gate, gate_ref[pl.ds(starts[k], BLOCK), :], transposed, preferred_element_type=f32
            ) + lax.dot_general(
                grad_up, up_ref[pl.ds(starts[k], BLOCK), :], transposed, preferred_element_type=f32
            )
            total = term if total is None else total + term

        @pl.when(step == 0)
        def _():
            acc[k] = total

        @pl.when(step == last)
        def _():
            outs[k][...] = (acc[k] + total).astype(outs[k].dtype)


def expert(place, pieces, own_weights, other_weights):
    count = len(pieces)
    rows = count * SLOTS
    whole = lambda shape: pl.BlockSpec(shape, lambda j: (0, 0))
    hidden = own_weights[0].shape[1]
    features = own_weights[0].shape[0]
    weight_specs = [
        pl.BlockSpec((features, HIDDEN_STEP), lambda j: (0, j)),
        pl.BlockSpec((features, HIDDEN_STEP), lambda j: (0, j)),
        pl.BlockSpec((HIDDEN_STEP, features), lambda j: (j, 0)),
    ]
    flat = [block for piece in pieces for block in piece]
    out_shape = [
        jax.ShapeDtypeStruct((rows, BLOCK), jnp.float32 if k == 0 else jnp.bfloat16) for k in range(4)
    ] + [jax.ShapeDtypeStruct((rows, 128), jnp.float32)]
    flops = 5 * 2 * rows * features * hidden * 2
    return pl.pallas_call(
        functools.partial(expert_body, count),
        grid=(hidden // HIDDEN_STEP,),
        in_specs=[pl.BlockSpec(memory_space=pltpu.SMEM)]
        + [whole(block.shape) for block in flat]
        + weight_specs
        + weight_specs,
        out_specs=[whole(s.shape) for s in out_shape],
        out_shape=out_shape,
        scratch_shapes=[
            pltpu.VMEM((4, rows, BLOCK), jnp.bfloat16),
            pltpu.VMEM((4, rows, BLOCK), jnp.bfloat16),
            pltpu.VMEM((4, rows, BLOCK), jnp.float32),
        ],
        compiler_params=pltpu.CompilerParams(vmem_limit_bytes=58 * 1024 * 1024),
        cost_estimate=pl.CostEstimate(
            flops=flops, bytes_accessed=6 * features * hidden * 2, transcendentals=rows * hidden * 2
        ),
        name="expert",
    )(place, *flat, *own_weights, *other_weights)


def local(
    layer_activations_input,
    output_gradient,
    specialist_choices_matrix,
    mixing_coefficients,
    quota_table,
    gating_matrix,
    widening_matrix,
    contracting_matrix,
):
    f32, bf16 = jnp.float32, jnp.bfloat16
    place = lax.axis_index("tp").astype(jnp.int32).reshape(1)
    own_weights = (gating_matrix, widening_matrix, contracting_matrix)
    other_weights = tuple(across_cores(w) for w in own_weights)

    numbers = seat_positions(specialist_choices_matrix, quota_table[0])
    row = jnp.arange(EXPERTS * 2 * CAP, dtype=jnp.int32)
    kind = (row // CAP) % 2
    seat = (row // (2 * CAP)) * PAD + row % CAP
    hit = jnp.any(numbers[None, :, :] == seat[:, None, None], axis=2)
    picker = jnp.concatenate(
        [hit & (kind == 0)[:, None], hit & (kind == 1)[:, None]], axis=1
    ).astype(bf16)
    both = jnp.concatenate([layer_activations_input, output_gradient], axis=0)
    payload = jnp.dot(picker, both, preferred_element_type=f32).astype(bf16)
    arrived = among_experts(payload.reshape(EXPERTS, 2 * CAP, BLOCK)).reshape(-1, BLOCK)
    goal = kind * SLOTS + (row // (2 * CAP)) * CAP + row % CAP
    sorter = (jnp.arange(2 * SLOTS, dtype=jnp.int32)[:, None] == goal[None, :]).astype(bf16)
    mine = jnp.dot(sorter, arrived, preferred_element_type=f32).astype(bf16)

    pieces = []
    for flip in range(4):
        own = mine if flip == 0 else along_z(mine, flip)
        left = along_x(own, 1)
        right = along_x(own, -1)
        far_x = along_x(left[:SLOTS], 1)
        far_d = along_x(right[SLOTS:], -1)
        pieces.append((own, left, right, far_x, far_d))

    sums = [None] * 4
    dots = [None] * 4
    for group in GROUPS:
        kept, to_left, to_right, to_far, lanes = expert(
            place, [pieces[flip] for flip in group], own_weights, other_weights
        )
        product = jnp.sum(lanes, axis=1).reshape(len(group), SLOTS)
        product = product + along_x(product, 1) + along_x(product, -1) + along_x(product, 2)
        total = (
            kept
            + along_x(to_right, 1).astype(f32)
            + along_x(to_left, -1).astype(f32)
            + along_x(to_far, 2).astype(f32)
        )
        for at, flip in enumerate(group):
            sums[flip] = total[at * SLOTS : (at + 1) * SLOTS]
            dots[flip] = product[at : at + 1]
    rows = sums[0]
    product = dots[0]
    for flip in range(1, 4):
        rows = rows + along_z(sums[flip].astype(bf16), flip).astype(f32)
        product = product + along_z(dots[flip], flip)

    product = product.reshape(EXPERTS, 1, CAP)
    high = product.astype(bf16)
    low = (product - high.astype(f32)).astype(bf16)
    tail = jnp.concatenate([high, low, jnp.zeros((EXPERTS, PAD - CAP - 2, CAP), bf16)], axis=1)
    tail = jnp.pad(tail, ((0, 0), (0, 0), (0, BLOCK - CAP)))
    home = among_experts(
        jnp.concatenate([rows.astype(bf16).reshape(EXPERTS, CAP, BLOCK), tail], axis=1)
    )
    slot_dot = home[:, CAP, :PAD].astype(f32) + home[:, CAP + 1, :PAD].astype(f32)
    slot_dot = slot_dot.reshape(-1)
    matches = numbers[None, :, :] == jnp.arange(EXPERTS * PAD, dtype=jnp.int32)[:, None, None]
    slot_weight = jnp.sum(jnp.where(matches, mixing_coefficients[None, :, :], 0.0), axis=2)
    token_sums = lax.dot_general(
        slot_weight,
        home.reshape(EXPERTS * PAD, BLOCK).astype(f32),
        (((0,), (0,)), ((), ())),
        precision=lax.Precision.HIGHEST,
        preferred_element_type=f32,
    )
    gate_grads = jnp.sum(jnp.where(matches, slot_dot[:, None, None], 0.0), axis=0)
    return (token_sums.astype(bf16), gate_grads)


def solution(mesh):
    in_specs = (
        P("ed", "tp"),
        P("ed", "tp"),
        P("ed", None),
        P("ed", None),
        P("ed", None),
        P(None, ("ed", "tp")),
        P(None, ("ed", "tp")),
        P(("ed", "tp"), None),
    )
    out_specs = (P("ed", "tp"), P("ed", None))
    return jax.shard_map(local, mesh=mesh, in_specs=in_specs, out_specs=out_specs, check_vma=False)
```

time: 535 us -> 202 us (0.38)
  blocking collectives: 397 us -> 14.7 us
  starting transfers between devices: 7.71 us -> 55.8 us
  waiting for transfers between devices: 60 us -> 89.9 us
  Pallas kernels: 0 us -> 27.4 us
  matrix products: 28.4 us -> 3.28 us
  local copies, waits for them, and re-layouts: 21.7 us -> 2.85 us
  between operations: 13.9 us -> 1.08 us
    all_to_all x3 -> x1, blocking collectives: 382 us -> 14.7 us  [among_experts(): lax.all_to_all(value, 'ed', split_axis=0, concat_axis=0, tiled=True, axis...]
    ppermute x0 -> x34, waiting for transfers between devices: none -> 74.7 us  [the longest x22 40.4 us: along_x(): return lax.ppermute(value, 'tp', [(i, (i + step) % 4) for i in range(4)])]
    all_gather x2 -> x0, waiting for transfers between devices: 50.5 us -> none  [the longest x1 47.2 us: local(): piece_d = lax.all_gather(rows_d, 'tp', axis=1, tiled=True)]
    ppermute x0 -> x34, starting transfers between devices: none -> 45.6 us  [the longest x22 33.6 us: along_x(): return lax.ppermute(value, 'tp', [(i, (i + step) % 4) for i in range(4)])]
    pallas_call x0 -> x1, Pallas kernels: none -> 27.4 us  [expert(): pl.pallas_call(functools.partial(expert_body, count), grid=(hidden // HID...]
    dot_general x8 -> x3, matrix products: 28.4 us -> 3.28 us  [the longest x1 2 us: local(): payload = jnp.dot(picker, both, preferred_element_type=f32).astype(bf16)]
    reshape x6 -> x3, local copies, waits for them, and re-layouts: 17.5 us -> 0.2 us  [the longest x1 0.09 us: local(): product = jnp.sum(lanes, axis=1).reshape(len(group), SLOTS)]
    unnamed x1 -> x0, blocking collectives: 15.5 us -> none
  transfers between devices with their start and end apart: 4 -> 35, of which waited for: 3 -> 20; matrix products, arithmetic and copies ran while one was open for 3% -> 3% of each run, Pallas kernels for 0% -> 0%
where the time goes in v1:
time: 202 us; the launch traced here: 201 us
  waiting for transfers between devices  89.9 us (45%)
  starting transfers between devices  55.8 us (28%)
  Pallas kernels  27.4 us (14%)
  blocking collectives  14.7 us (7%)
  other arithmetic  5.86 us (3%)
  matrix products  3.28 us (2%)
  local copies, waits for them, and re-layouts  2.85 us (1%)
    ppermute x22, waiting for transfers between devices, along_x(): return lax.ppermute(value, 'tp', [(i, (i + step) % 4) for i in range(4)])  40.4 us
    ppermute x9, waiting for transfers between devices, along_z(): return lax.ppermute(value, 'ed', [(i, i ^ flip * 2) for i in range(64)])  34.2 us
    ppermute x22, starting transfers between devices, along_x(): return lax.ppermute(value, 'tp', [(i, (i + step) % 4) for i in range(4)])  33.6 us
    pallas_call x1, Pallas kernels, expert(): pl.pallas_call(functools.partial(expert_body, count), grid=(hidden // HID...  27.4 us
    all_to_all x1, waiting for transfers between devices, among_experts(): lax.all_to_all(value, 'ed', split_axis=0, concat_axis=0, tiled=True, axis...  15.3 us
    all_to_all x1, blocking collectives, among_experts(): lax.all_to_all(value, 'ed', split_axis=0, concat_axis=0, tiled=True, axis...  14.7 us
    ppermute x9, starting transfers between devices, along_z(): return lax.ppermute(value, 'ed', [(i, i ^ flip * 2) for i in range(64)])  11.2 us
    all_to_all x1, starting transfers between devices, among_experts(): lax.all_to_all(value, 'ed', split_axis=0, concat_axis=0, tiled=True, axis...  10.2 us
  transfers between devices with their start and end apart: 35, of which 20 were waited for; matrix products, arithmetic and copies ran while one was open for 3% of the time, Pallas kernels for 0%

profile of v1, /device:TPU:32, one launch (start us, length us, event | category | flops | bytes accessed | tf_op | source)
XLA Modules:
  0.0 200.9 jit_solution(4669076847007523577)
XLA Ops:
  7.4 10.2 %all-to-all-start = ((bf16[8,24,768]{2,1,0:T(8,128)(2,1)}), bf16[8,24,768]{2,1,0:T(8,128)(2,1)S(1)}, u32[]{:S(2)}, u32[]{:S(2)}) async-start(bf16[8,24,768]{2,1,0:T(8,128)(2,1)} %bitcast.4), calls=%async_computation | async-start | bytes 589824 | tf_op jit(solution)/shard_map/all_to_all | solution.py:43
  17.6 15.3 %all-to-all-done = bf16[8,24,768]{2,1,0:T(8,128)(2,1)S(1)} async-done(((bf16[8,24,768]{2,1,0:T(8,128)(2,1)}), bf16[8,24,768]{2,1,0:T(8,128)(2,1)S(1)}, u32[]{:S(2)}, u32[]{:S(2)}) %all-to-all-start) | async-done | bytes 294944 | tf_op jit(solution)/shard_map/all_to_all | solution.py:43
  34.8 10.8 %collective-permute-done.9.refs_10_ = bf16[192,768]{1,0:T(8,128)(2,1)S(1)} collective-permute-done((bf16[192,768]{1,0:T(8,128)(2,1)S(1)}, bf16[192,768]{1,0:T(8,128)(2,1)S(1)}, u32[]{:S(2)}, u32[]{:S(2)}) %collective-permute-start.9) | collective-permute-done | bytes 294944 | tf_op jit(solution)/shard_map/ppermute | solution.py:34
  49.4 4.1 %collective-permute-done.1.refs_2_ = bf16[192,768]{1,0:T(8,128)(2,1)S(1)} collective-permute-done((bf16[192,768]{1,0:T(8,128)(2,1)S(1)}, bf16[192,768]{1,0:T(8,128)(2,1)S(1)}, u32[]{:S(2)}, u32[]{:S(2)}) %collective-permute-start.1) | collective-permute-done | bytes 294944 | tf_op jit(solution)/shard_map/ppermute | solution.py:30
  53.5 2.9 %collective-permute-start.4 = (bf16[192,768]{1,0:T(8,128)(2,1)S(1)}, bf16[192,768]{1,0:T(8,128)(2,1)S(1)}, u32[]{:S(2)}, u32[]{:S(2)}) collective-permute-start(bf16[192,768]{1,0:T(8,128)(2,1)S(1)} %convolution_convert_fusion.refs_0_), channel_id=1, source_target_pairs={{0,8},{4,12},{8,0},{12,4},{16,24},{20,28},{24,16},{28,20},{32,40},... | collective-permute-start | bytes 884744 | tf_op jit(solution)/shard_map/ppermute | solution.py:34
  56.4 5.6 %collective-permute-done.14.refs_15_ = bf16[192,768]{1,0:T(8,128)(2,1)S(1)} collective-permute-done((bf16[192,768]{1,0:T(8,128)(2,1)S(1)}, bf16[192,768]{1,0:T(8,128)(2,1)S(1)}, u32[]{:S(2)}, u32[]{:S(2)}) %collective-permute-start.14) | collective-permute-done | bytes 294944 | tf_op jit(solution)/shard_map/ppermute | solution.py:34
  62.0 2.9 %collective-permute-done.4.refs_5_ = bf16[192,768]{1,0:T(8,128)(2,1)S(1)} collective-permute-done((bf16[192,768]{1,0:T(8,128)(2,1)S(1)}, bf16[192,768]{1,0:T(8,128)(2,1)S(1)}, u32[]{:S(2)}, u32[]{:S(2)}) %collective-permute-start.4) | collective-permute-done | bytes 294944 | tf_op jit(solution)/shard_map/ppermute | solution.py:34
  65.7 3.8 %collective-permute-done.2.refs_3_ = bf16[96,768]{1,0:T(8,128)(2,1)S(1)} collective-permute-done((bf16[96,768]{1,0:T(8,128)(2,1)S(1)}, bf16[96,768]{1,0:T(8,128)(2,1)S(1)}, u32[]{:S(2)}, u32[]{:S(2)}) %collective-permute-start.2) | collective-permute-done | bytes 147488 | tf_op jit(solution)/shard_map/ppermute | solution.py:30
  72.7 7.0 %collective-permute-done.10.refs_11_ = bf16[192,768]{1,0:T(8,128)(2,1)S(1)} collective-permute-done((bf16[192,768]{1,0:T(8,128)(2,1)S(1)}, bf16[192,768]{1,0:T(8,128)(2,1)S(1)}, u32[]{:S(2)}, u32[]{:S(2)}) %collective-permute-start.10) | collective-permute-done | bytes 294944 | tf_op jit(solution)/shard_map/ppermute | solution.py:30
  79.7 3.2 %collective-permute-start.16 = (bf16[192,768]{1,0:T(8,128)(2,1)S(1)}, bf16[192,768]{1,0:T(8,128)(2,1)S(1)}, u32[]{:S(2)}, u32[]{:S(2)}) collective-permute-start(bf16[192,768]{1,0:T(8,128)(2,1)S(1)} %collective-permute-done.14.refs_15_), channel_id=1, source_target_pairs={{0,3},{1,0},{2,1},{3,2},{4,7},{5,4},{6,5},{7,6},{8,11},{9,8},{10,9... | collective-permute-start | bytes 884744 | tf_op jit(solution)/shard_map/ppermute | solution.py:30
  82.9 7.6 %collective-permute-done.15.refs_16_ = bf16[192,768]{1,0:T(8,128)(2,1)S(1)} collective-permute-done((bf16[192,768]{1,0:T(8,128)(2,1)S(1)}, bf16[192,768]{1,0:T(8,128)(2,1)S(1)}, u32[]{:S(2)}, u32[]{:S(2)}) %collective-permute-start.15) | collective-permute-done | bytes 294944 | tf_op jit(solution)/shard_map/ppermute | solution.py:30
  90.5 3.5 %collective-permute-start.6 = (bf16[192,768]{1,0:T(8,128)(2,1)S(1)}, bf16[192,768]{1,0:T(8,128)(2,1)S(1)}, u32[]{:S(2)}, u32[]{:S(2)}) collective-permute-start(bf16[192,768]{1,0:T(8,128)(2,1)S(1)} %collective-permute-done.4.refs_5_), channel_id=1, source_target_pairs={{0,3},{1,0},{2,1},{3,2},{4,7},{5,4},{6,5},{7,6},{8,11},{9,8},{10,9... | collective-permute-start | bytes 884744 | tf_op jit(solution)/shard_map/ppermute | solution.py:30
  94.0 4.9 %collective-permute-done.5.refs_6_ = bf16[192,768]{1,0:T(8,128)(2,1)S(1)} collective-permute-done((bf16[192,768]{1,0:T(8,128)(2,1)S(1)}, bf16[192,768]{1,0:T(8,128)(2,1)S(1)}, u32[]{:S(2)}, u32[]{:S(2)}) %collective-permute-start.5) | collective-permute-done | bytes 294944 | tf_op jit(solution)/shard_map/ppermute | solution.py:30
  98.9 3.3 %collective-permute-start.13 = (bf16[96,768]{1,0:T(8,128)(2,1)S(1)}, bf16[96,768]{1,0:T(8,128)(2,1)S(1)}, u32[]{:S(2)}, u32[]{:S(2)}) collective-permute-start(bf16[96,768]{1,0:T(8,128)(2,1)S(1)} %slice.89), channel_id=1, source_target_pairs={{0,3},{1,0},{2,1},{3,2},{4,7},{5,4},{6,5},{7,6},{8,11},{9,8},{10,9... | collective-permute-start | bytes 442376 | tf_op jit(solution)/shard_map/ppermute | solution.py:30
  102.3 3.0 %collective-permute-done.12.refs_13_ = bf16[96,768]{1,0:T(8,128)(2,1)S(1)} collective-permute-done((bf16[96,768]{1,0:T(8,128)(2,1)S(1)}, bf16[96,768]{1,0:T(8,128)(2,1)S(1)}, u32[]{:S(2)}, u32[]{:S(2)}) %collective-permute-start.12) | collective-permute-done | bytes 147488 | tf_op jit(solution)/shard_map/ppermute | solution.py:30
  105.3 3.6 %collective-permute-start.18 = (bf16[96,768]{1,0:T(8,128)(2,1)S(1)}, bf16[96,768]{1,0:T(8,128)(2,1)S(1)}, u32[]{:S(2)}, u32[]{:S(2)}) collective-permute-start(bf16[96,768]{1,0:T(8,128)(2,1)S(1)} %slice.91), channel_id=1, source_target_pairs={{0,3},{1,0},{2,1},{3,2},{4,7},{5,4},{6,5},{7,6},{8,11},{9,8},{10,9... | collective-permute-start | bytes 442376 | tf_op jit(solution)/shard_map/ppermute | solution.py:30
  111.6 3.6 %collective-permute-start.8 = (bf16[96,768]{1,0:T(8,128)(2,1)S(1)}, bf16[96,768]{1,0:T(8,128)(2,1)S(1)}, u32[]{:S(2)}, u32[]{:S(2)}) collective-permute-start(bf16[96,768]{1,0:T(8,128)(2,1)S(1)} %slice.87), channel_id=1, source_target_pairs={{0,3},{1,0},{2,1},{3,2},{4,7},{5,4},{6,5},{7,6},{8,11},{9,8},{10,9... | collective-permute-start | bytes 442376 | tf_op jit(solution)/shard_map/ppermute | solution.py:30
  118.7 27.4 %expert.1 = (f32[384,768]{1,0:T(8,128)}, bf16[384,768]{1,0:T(8,128)(2,1)}, bf16[384,768]{1,0:T(8,128)(2,1)}, bf16[384,768]{1,0:T(8,128)(2,1)}, f32[384,128]{1,0:T(8,128)}) custom-call(s32[1]{0:T(128)} %bitcast.3.place_ref, bf16[192,768]{1,0:T(8,128)(2,1)} %copy-done, bf16[192,768]{1,0:T(8,128)(2,1)} %copy-done.1, bf16[192,768]{1,0:T(8,128)(2,1)} %copy-done.2, ...), custom_call_target="tpu_custom_call" | custom-call | flops 12079595520 | bytes 18874368 | tf_op jit(solution)/shard_map/expert/pallas_call | solution.py:140
  147.5 3.6 %collective-permute-start.29 = (f32[4,96]{1,0:T(4,128)S(1)}, f32[4,96]{1,0:T(4,128)S(1)}, u32[]{:S(2)}, u32[]{:S(2)}) collective-permute-start(f32[4,96]{1,0:T(4,128)S(1)} %reshape.200), channel_id=1, source_target_pairs={{0,3},{1,0},{2,1},{3,2},{4,7},{5,4},{6,5},{7,6},{8,11},{9,8},{10,9... | collective-permute-start | bytes 4616 | tf_op jit(solution)/shard_map/ppermute | solution.py:30
  161.5 5.1 %collective-permute-done.33 = f32[1,96]{1,0:T(1,128)S(1)} collective-permute-done((f32[1,96]{1,0:T(1,128)S(1)}, f32[1,96]{1,0:T(1,128)S(1)}, u32[]{:S(2)}, u32[]{:S(2)}) %collective-permute-start.33) | collective-permute-done | bytes 416 | tf_op jit(solution)/shard_map/ppermute | solution.py:34
  166.7 3.4 %collective-permute-done.22 = bf16[384,768]{1,0:T(8,128)(2,1)S(1)} collective-permute-done((bf16[384,768]{1,0:T(8,128)(2,1)}, bf16[384,768]{1,0:T(8,128)(2,1)S(1)}, u32[]{:S(2)}, u32[]{:S(2)}) %collective-permute-start.22) | collective-permute-done | bytes 589856 | tf_op jit(solution)/shard_map/ppermute | solution.py:30
  177.0 4.2 %collective-permute-done.26 = bf16[96,768]{1,0:T(8,128)(2,1)S(1)} collective-permute-done((bf16[96,768]{1,0:T(8,128)(2,1)S(1)}, bf16[96,768]{1,0:T(8,128)(2,1)S(1)}, u32[]{:S(2)}, u32[]{:S(2)}) %collective-permute-start.26) | collective-permute-done | bytes 147488 | tf_op jit(solution)/shard_map/ppermute | solution.py:34
  181.2 3.0 %collective-permute-done.27 = bf16[96,768]{1,0:T(8,128)(2,1)S(1)} collective-permute-done((bf16[96,768]{1,0:T(8,128)(2,1)S(1)}, bf16[96,768]{1,0:T(8,128)(2,1)S(1)}, u32[]{:S(2)}, u32[]{:S(2)}) %collective-permute-start.27) | collective-permute-done | bytes 147488 | tf_op jit(solution)/shard_map/ppermute | solution.py:34
  184.4 14.7 %all_to_all.10 = bf16[8,16,768]{2,1,0:T(8,128)(2,1)S(1)} all-to-all(bf16[8,16,768]{2,1,0:T(8,128)(2,1)S(1)} %fusion.7), channel_id=1, replica_groups={{0,32,64,96,128,160,192,224},{4,36,68,100,132,164,196,228},{8,40,72,104..., dimensions={0} | all-to-all | bytes 393216 | tf_op jit(solution)/shard_map/all_to_all | solution.py:43
  (139 shorter events, 43.3 us)
Async XLA Ops:
  0.6 117.4 %collective-permute-start.19 = (bf16[3072,512]{1,0:T(8,128)(2,1)}, bf16[3072,512]{1,0:T(8,128)(2,1)}, u32[]{:S(2)}, u32[]{:S(2)}) collective-permute-start(bf16[3072,512]{1,0:T(8,128)(2,1)} %refs_20_.1), channel_id=1, source_target_pairs={{0,4},{4,0},{8,12},{12,8},{16,20},{20,16},{24,28},{28,24},{32,36},... | collective-permute-start | bytes 9437192 | tf_op jit(solution)/shard_map/ppermute | solution.py:38
  0.7 117.3 %collective-permute-start.20 = (bf16[3072,512]{1,0:T(8,128)(2,1)}, bf16[3072,512]{1,0:T(8,128)(2,1)}, u32[]{:S(2)}, u32[]{:S(2)}) collective-permute-start(bf16[3072,512]{1,0:T(8,128)(2,1)} %refs_21_.1), channel_id=1, source_target_pairs={{0,4},{4,0},{8,12},{12,8},{16,20},{20,16},{24,28},{28,24},{32,36},... | collective-permute-start | bytes 9437192 | tf_op jit(solution)/shard_map/ppermute | solution.py:38
  1.2 116.8 %collective-permute-start.21 = (bf16[512,3072]{1,0:T(8,128)(2,1)}, bf16[512,3072]{1,0:T(8,128)(2,1)}, u32[]{:S(2)}, u32[]{:S(2)}) collective-permute-start(bf16[512,3072]{1,0:T(8,128)(2,1)} %refs_22_.1), channel_id=1, source_target_pairs={{0,4},{4,0},{8,12},{12,8},{16,20},{20,16},{24,28},{28,24},{32,36},... | collective-permute-start | bytes 9437192 | tf_op jit(solution)/shard_map/ppermute | solution.py:38
  7.4 25.5 %all-to-all-start = ((bf16[8,24,768]{2,1,0:T(8,128)(2,1)}), bf16[8,24,768]{2,1,0:T(8,128)(2,1)S(1)}, u32[]{:S(2)}, u32[]{:S(2)}) async-start(bf16[8,24,768]{2,1,0:T(8,128)(2,1)} %bitcast.4), calls=%async_computation | async-start | bytes 589824 | tf_op jit(solution)/shard_map/all_to_all | solution.py:43
  33.1 12.4 %collective-permute-start.9 = (bf16[192,768]{1,0:T(8,128)(2,1)S(1)}, bf16[192,768]{1,0:T(8,128)(2,1)S(1)}, u32[]{:S(2)}, u32[]{:S(2)}) collective-permute-start(bf16[192,768]{1,0:T(8,128)(2,1)S(1)} %convolution_convert_fusion.refs_0_), channel_id=1, source_target_pairs={{0,16},{4,20},{8,24},{12,28},{16,0},{20,4},{24,8},{28,12},{32,48},... | collective-permute-start | bytes 884744 | tf_op jit(solution)/shard_map/ppermute | solution.py:34
  33.2 15.1 %collective-permute-start = (bf16[192,768]{1,0:T(8,128)(2,1)S(1)}, bf16[192,768]{1,0:T(8,128)(2,1)S(1)}, u32[]{:S(2)}, u32[]{:S(2)}) collective-permute-start(bf16[192,768]{1,0:T(8,128)(2,1)S(1)} %convolution_convert_fusion.refs_0_), channel_id=1, source_target_pairs={{0,1},{1,2},{2,3},{3,0},{4,5},{5,6},{6,7},{7,4},{8,9},{9,10},{10,1... | collective-permute-start | bytes 884744 | tf_op jit(solution)/shard_map/ppermute | solution.py:30
  45.6 7.9 %collective-permute-start.1 = (bf16[192,768]{1,0:T(8,128)(2,1)S(1)}, bf16[192,768]{1,0:T(8,128)(2,1)S(1)}, u32[]{:S(2)}, u32[]{:S(2)}) collective-permute-start(bf16[192,768]{1,0:T(8,128)(2,1)S(1)} %convolution_convert_fusion.refs_0_), channel_id=1, source_target_pairs={{0,3},{1,0},{2,1},{3,2},{4,7},{5,4},{6,5},{7,6},{8,11},{9,8},{10,9... | collective-permute-start | bytes 884744 | tf_op jit(solution)/shard_map/ppermute | solution.py:30
  48.3 13.6 %collective-permute-start.14 = (bf16[192,768]{1,0:T(8,128)(2,1)S(1)}, bf16[192,768]{1,0:T(8,128)(2,1)S(1)}, u32[]{:S(2)}, u32[]{:S(2)}) collective-permute-start(bf16[192,768]{1,0:T(8,128)(2,1)S(1)} %convolution_convert_fusion.refs_0_), channel_id=1, source_target_pairs={{0,24},{4,28},{8,16},{12,20},{16,8},{20,12},{24,0},{28,4},{32,56},... | collective-permute-start | bytes 884744 | tf_op jit(solution)/shard_map/ppermute | solution.py:34
  53.5 11.4 %collective-permute-start.4 = (bf16[192,768]{1,0:T(8,128)(2,1)S(1)}, bf16[192,768]{1,0:T(8,128)(2,1)S(1)}, u32[]{:S(2)}, u32[]{:S(2)}) collective-permute-start(bf16[192,768]{1,0:T(8,128)(2,1)S(1)} %convolution_convert_fusion.refs_0_), channel_id=1, source_target_pairs={{0,8},{4,12},{8,0},{12,4},{16,24},{20,28},{24,16},{28,20},{32,40},... | collective-permute-start | bytes 884744 | tf_op jit(solution)/shard_map/ppermute | solution.py:34
  62.0 7.5 %collective-permute-start.2 = (bf16[96,768]{1,0:T(8,128)(2,1)S(1)}, bf16[96,768]{1,0:T(8,128)(2,1)S(1)}, u32[]{:S(2)}, u32[]{:S(2)}) collective-permute-start(bf16[96,768]{1,0:T(8,128)(2,1)S(1)} %slice.84), channel_id=1, source_target_pairs={{0,1},{1,2},{2,3},{3,0},{4,5},{5,6},{6,7},{7,4},{8,9},{9,10},{10,1... | collective-permute-start | bytes 442376 | tf_op jit(solution)/shard_map/ppermute | solution.py:30
  69.5 10.2 %collective-permute-start.10 = (bf16[192,768]{1,0:T(8,128)(2,1)S(1)}, bf16[192,768]{1,0:T(8,128)(2,1)S(1)}, u32[]{:S(2)}, u32[]{:S(2)}) collective-permute-start(bf16[192,768]{1,0:T(8,128)(2,1)S(1)} %collective-permute-done.9.refs_10_), channel_id=1, source_target_pairs={{0,1},{1,2},{2,3},{3,0},{4,5},{5,6},{6,7},{7,4},{8,9},{9,10},{10,1... | collective-permute-start | bytes 884744 | tf_op jit(solution)/shard_map/ppermute | solution.py:30
  70.0 9.7 %collective-permute-start.11 = (bf16[192,768]{1,0:T(8,128)(2,1)S(1)}, bf16[192,768]{1,0:T(8,128)(2,1)S(1)}, u32[]{:S(2)}, u32[]{:S(2)}) collective-permute-start(bf16[192,768]{1,0:T(8,128)(2,1)S(1)} %collective-permute-done.9.refs_10_), channel_id=1, source_target_pairs={{0,3},{1,0},{2,1},{3,2},{4,7},{5,4},{6,5},{7,6},{8,11},{9,8},{10,9... | collective-permute-start | bytes 884744 | tf_op jit(solution)/shard_map/ppermute | solution.py:30
  79.7 10.8 %collective-permute-start.15 = (bf16[192,768]{1,0:T(8,128)(2,1)S(1)}, bf16[192,768]{1,0:T(8,128)(2,1)S(1)}, u32[]{:S(2)}, u32[]{:S(2)}) collective-permute-start(bf16[192,768]{1,0:T(8,128)(2,1)S(1)} %collective-permute-done.14.refs_15_), channel_id=1, source_target_pairs={{0,1},{1,2},{2,3},{3,0},{4,5},{5,6},{6,7},{7,4},{8,9},{9,10},{10,1... | collective-permute-start | bytes 884744 | tf_op jit(solution)/shard_map/ppermute | solution.py:30
  79.7 10.8 %collective-permute-start.16 = (bf16[192,768]{1,0:T(8,128)(2,1)S(1)}, bf16[192,768]{1,0:T(8,128)(2,1)S(1)}, u32[]{:S(2)}, u32[]{:S(2)}) collective-permute-start(bf16[192,768]{1,0:T(8,128)(2,1)S(1)} %collective-permute-done.14.refs_15_), channel_id=1, source_target_pairs={{0,3},{1,0},{2,1},{3,2},{4,7},{5,4},{6,5},{7,6},{8,11},{9,8},{10,9... | collective-permute-start | bytes 884744 | tf_op jit(solution)/shard_map/ppermute | solution.py:30
  90.5 8.4 %collective-permute-start.5 = (bf16[192,768]{1,0:T(8,128)(2,1)S(1)}, bf16[192,768]{1,0:T(8,128)(2,1)S(1)}, u32[]{:S(2)}, u32[]{:S(2)}) collective-permute-start(bf16[192,768]{1,0:T(8,128)(2,1)S(1)} %collective-permute-done.4.refs_5_), channel_id=1, source_target_pairs={{0,1},{1,2},{2,3},{3,0},{4,5},{5,6},{6,7},{7,4},{8,9},{9,10},{10,1... | collective-permute-start | bytes 884744 | tf_op jit(solution)/shard_map/ppermute | solution.py:30
  90.5 8.4 %collective-permute-start.6 = (bf16[192,768]{1,0:T(8,128)(2,1)S(1)}, bf16[192,768]{1,0:T(8,128)(2,1)S(1)}, u32[]{:S(2)}, u32[]{:S(2)}) collective-permute-start(bf16[192,768]{1,0:T(8,128)(2,1)S(1)} %collective-permute-done.4.refs_5_), channel_id=1, source_target_pairs={{0,3},{1,0},{2,1},{3,2},{4,7},{5,4},{6,5},{7,6},{8,11},{9,8},{10,9... | collective-permute-start | bytes 884744 | tf_op jit(solution)/shard_map/ppermute | solution.py:30
  105.3 6.4 %collective-permute-start.17 = (bf16[96,768]{1,0:T(8,128)(2,1)S(1)}, bf16[96,768]{1,0:T(8,128)(2,1)S(1)}, u32[]{:S(2)}, u32[]{:S(2)}) collective-permute-start(bf16[96,768]{1,0:T(8,128)(2,1)S(1)} %slice.90), channel_id=1, source_target_pairs={{0,1},{1,2},{2,3},{3,0},{4,5},{5,6},{6,7},{7,4},{8,9},{9,10},{10,1... | collective-permute-start | bytes 442376 | tf_op jit(solution)/shard_map/ppermute | solution.py:30
  147.3 9.2 %collective-permute-start.28 = (f32[4,96]{1,0:T(4,128)S(1)}, f32[4,96]{1,0:T(4,128)S(1)}, u32[]{:S(2)}, u32[]{:S(2)}) collective-permute-start(f32[4,96]{1,0:T(4,128)S(1)} %reshape.200), channel_id=1, source_target_pairs={{0,1},{1,2},{2,3},{3,0},{4,5},{5,6},{6,7},{7,4},{8,9},{9,10},{10,1... | collective-permute-start | bytes 4616 | tf_op jit(solution)/shard_map/ppermute | solution.py:30
  147.5 9.2 %collective-permute-start.29 = (f32[4,96]{1,0:T(4,128)S(1)}, f32[4,96]{1,0:T(4,128)S(1)}, u32[]{:S(2)}, u32[]{:S(2)}) collective-permute-start(f32[4,96]{1,0:T(4,128)S(1)} %reshape.200), channel_id=1, source_target_pairs={{0,3},{1,0},{2,1},{3,2},{4,7},{5,4},{6,5},{7,6},{8,11},{9,8},{10,9... | collective-permute-start | bytes 4616 | tf_op jit(solution)/shard_map/ppermute | solution.py:30
  152.5 17.6 %collective-permute-start.22 = (bf16[384,768]{1,0:T(8,128)(2,1)}, bf16[384,768]{1,0:T(8,128)(2,1)S(1)}, u32[]{:S(2)}, u32[]{:S(2)}) collective-permute-start(bf16[384,768]{1,0:T(8,128)(2,1)} %get-tuple-element.8), channel_id=1, source_target_pairs={{0,1},{1,2},{2,3},{3,0},{4,5},{5,6},{6,7},{7,4},{8,9},{9,10},{10,1... | collective-permute-start | bytes 1769480 | tf_op jit(solution)/shard_map/ppermute | solution.py:30
  153.9 16.2 %collective-permute-start.23 = (bf16[384,768]{1,0:T(8,128)(2,1)}, bf16[384,768]{1,0:T(8,128)(2,1)S(1)}, u32[]{:S(2)}, u32[]{:S(2)}) collective-permute-start(bf16[384,768]{1,0:T(8,128)(2,1)} %get-tuple-element.9), channel_id=1, source_target_pairs={{0,3},{1,0},{2,1},{3,2},{4,7},{5,4},{6,5},{7,6},{8,11},{9,8},{10,9... | collective-permute-start | bytes 1769480 | tf_op jit(solution)/shard_map/ppermute | solution.py:30
  156.5 13.7 %collective-permute-start.24 = (bf16[384,768]{1,0:T(8,128)(2,1)}, bf16[384,768]{1,0:T(8,128)(2,1)S(1)}, u32[]{:S(2)}, u32[]{:S(2)}) collective-permute-start(bf16[384,768]{1,0:T(8,128)(2,1)} %get-tuple-element.10), channel_id=1, source_target_pairs={{0,2},{1,3},{2,0},{3,1},{4,6},{5,7},{6,4},{7,5},{8,10},{9,11},{10,... | collective-permute-start | bytes 1769480 | tf_op jit(solution)/shard_map/ppermute | solution.py:30
  171.8 9.4 %collective-permute-start.26 = (bf16[96,768]{1,0:T(8,128)(2,1)S(1)}, bf16[96,768]{1,0:T(8,128)(2,1)S(1)}, u32[]{:S(2)}, u32[]{:S(2)}) collective-permute-start(bf16[96,768]{1,0:T(8,128)(2,1)S(1)} %get-tuple-element.20), channel_id=1, source_target_pairs={{0,16},{4,20},{8,24},{12,28},{16,0},{20,4},{24,8},{28,12},{32,48},... | collective-permute-start | bytes 442376 | tf_op jit(solution)/shard_map/ppermute | solution.py:34
  174.3 9.9 %collective-permute-start.27 = (bf16[96,768]{1,0:T(8,128)(2,1)S(1)}, bf16[96,768]{1,0:T(8,128)(2,1)S(1)}, u32[]{:S(2)}, u32[]{:S(2)}) collective-permute-start(bf16[96,768]{1,0:T(8,128)(2,1)S(1)} %get-tuple-element.19), channel_id=1, source_target_pairs={{0,24},{4,28},{8,16},{12,20},{16,8},{20,12},{24,0},{28,4},{32,56},... | collective-permute-start | bytes 442376 | tf_op jit(solution)/shard_map/ppermute | solution.py:34
  (32 other events, 708.6 us)
